TPU v7x, 32 devices: a whole 2x2x4 slice. The times are simulated.
32 devices in a mesh: fx: 8 (over z, x), fy: 4 (over y, core).
Axes of the slice: x: 2, y: 2, z: 4, core: 2. Of those that a mesh axis runs over, the one named last changes fastest.
Arguments:
- air_state: float32 [2, 58, 128, 2048], P(None, None, 'fy', 'fx'), may hold values from -6 to 6
- jacobian: float32 [128, 2048], P('fy', 'fx'), may hold values from 0.5 to 2
- viscosity: float32 [128, 2048], P('fy', 'fx'), may hold values from 0.5 to 2
- mixing: float32 [58, 58], replicated, may hold values from -0.75 to 0.75
- convect_dest: int32 [128, 8], P('fy', 'fx'), may hold values from -1 to 7, as said below
Outputs:
- next_state: float32 [2, 58, 128, 2048], P(None, None, 'fy', 'fx')
Inputs may be any that keep to these rules, and one draw needn't show every extreme that they name: `convect_dest`: in each fy row of devices, 2 devices have all their blocks convective and the others none; every fx index of that row is named by exactly 8 blocks of the row, and at most 4 blocks of one device name the same index.
All inputs are finite; a program needn't handle non-finite values.
Results may differ from a plain program's by a relative error of at most 0.00089.
Values may be sent and summed in bfloat16 or wider, within the bound.
A program may use at most 64 MiB of HBM per device.

v0:
```python
import jax
import jax.numpy as jnp
import numpy as np
from jax import lax
from jax.sharding import PartitionSpec as P

SUBSTEPS = 24


def padded_2(block, sides, width):
    for axis, dim in sides:
        count = lax.axis_size(axis)
        forward = [(i, i + 1) for i in range(count - 1)]
        forward.append((count - 1, 0))
        backward = [(target, source) for source, target in forward]
        low = lax.ppermute(
            lax.slice_in_dim(block, block.shape[dim] - width, None, axis=dim), axis, forward
        )
        high = lax.ppermute(lax.slice_in_dim(block, 0, width, axis=dim), axis, backward)
        block = jnp.concatenate([low, block, high], axis=dim)
    return block


def gll_tables():
    nodes = np.array([-1.0, -1.0 / np.sqrt(5.0), 1.0 / np.sqrt(5.0), 1.0])
    gll_weight = np.array([1.0 / 6.0, 5.0 / 6.0, 5.0 / 6.0, 1.0 / 6.0])
    deriv = np.zeros((4, 4))
    for first in range(4):
        for second in range(4):
            if first == second:
                deriv[first, second] = sum(
                    (1.0 / (nodes[first] - nodes[other]) for other in range(4) if other != first)
                )
            else:
                top = np.prod([nodes[first] - nodes[other] for other in range(4) if other != first])
                below = np.prod(
                    [nodes[second] - nodes[other] for other in range(4) if other != second]
                )
                deriv[first, second] = top / below / (nodes[first] - nodes[second])
    stiff = deriv.T * gll_weight[None, :] @ deriv
    return (stiff, gll_weight)


def column_physics(temper, moist, mixing, pattern):
    start_t, start_q = (temper, moist)

    def substep(index, carry):
        temper_now, moist_now = carry
        cond = jax.nn.softplus(moist_now - 0.5 * temper_now)
        temper_now = temper_now + 0.25 * jnp.einsum(
            pattern, mixing, cond, precision=lax.Precision.HIGHEST
        )
        moist_now = moist_now - 0.25 * cond
        return (temper_now, moist_now)

    temper, moist = lax.fori_loop(0, SUBSTEPS, substep, (temper, moist))
    return (temper - start_t, moist - start_q)


def partner_sum(values, padded, index_vec, axis_pos):
    count = values.shape[axis_pos]
    upper = lax.slice_in_dim(padded, 2, count + 2, axis=axis_pos)
    lower = lax.slice_in_dim(padded, 0, count, axis=axis_pos)
    return values + jnp.where(index_vec == 3, upper, jnp.where(index_vec == 0, lower, 0.0))


def body(air_state, jacobian, viscosity, mixing, convect_dest):
    high = lax.Precision.HIGHEST
    levels, row_count, col_count = (air_state.shape[1], air_state.shape[2], air_state.shape[3])
    stiff, gll_weight = gll_tables()
    along_mat = jnp.asarray(np.kron(np.eye(col_count // 4), stiff), jnp.float32)
    across_mat = jnp.asarray(np.kron(np.eye(row_count // 4), stiff), jnp.float32)
    weight_rows = jnp.asarray(np.tile(gll_weight, row_count // 4), jnp.float32)
    weight_cols = jnp.asarray(np.tile(gll_weight, col_count // 4), jnp.float32)
    col_index = jnp.arange(col_count) % 4
    row_index = (jnp.arange(row_count) % 4)[:, None]
    snap_half = air_state.astype(jnp.bfloat16)
    dest_dev = convect_dest[:, 0]
    slab_count = lax.axis_size("fx")
    cap = max(1, row_count // slab_count)
    keep = row_count // 4
    order = jnp.arange(row_count)
    earlier = (dest_dev[:, None] == dest_dev[None, :]) & (order[None, :] < order[:, None])
    rank = jnp.sum(earlier.astype(jnp.int32), axis=1)
    slot = jnp.where(dest_dev >= 0, dest_dev * cap + rank, -1)
    pick = jnp.arange(slab_count * cap)[:, None] == slot[None, :]
    packed = jnp.einsum(
        "sb,kbx->skx",
        pick.astype(jnp.bfloat16),
        snap_half.reshape(2 * levels, row_count, col_count),
        preferred_element_type=jnp.float32,
    )
    packed = packed.astype(jnp.bfloat16).reshape(slab_count, cap, 2 * levels, col_count)
    live = jnp.any(pick, axis=1).astype(jnp.int32).reshape(slab_count, cap)
    arrived, arrived_live = (
        lax.all_to_all(packed, "fx", split_axis=0, concat_axis=0, tiled=True),
        lax.all_to_all(live, "fx", split_axis=0, concat_axis=0, tiled=True),
    )
    flat_live = arrived_live.reshape(-1)
    live_rank = jnp.cumsum(flat_live) - 1
    select = (flat_live[None, :] == 1) & (live_rank[None, :] == jnp.arange(keep)[:, None])
    work = jnp.einsum(
        "rs,skx->rkx",
        select.astype(jnp.bfloat16),
        arrived.reshape(slab_count * cap, 2 * levels, col_count),
        preferred_element_type=jnp.float32,
    )
    tend_t, tend_q = column_physics(work[:, :levels], work[:, levels:], mixing, "lm,bmx->blx")
    tendency = jnp.concatenate([tend_t, tend_q], axis=1)
    back_slots = jnp.einsum("rs,rkx->skx", select.astype(jnp.float32), tendency, precision=high)
    returned = lax.all_to_all(
        back_slots.reshape(slab_count, cap, 2 * levels, col_count),
        "fx",
        split_axis=0,
        concat_axis=0,
        tiled=True,
    )
    physics = jnp.einsum(
        "sb,skx->kbx",
        pick.astype(jnp.float32),
        returned.reshape(slab_count * cap, 2 * levels, col_count),
        precision=high,
    )
    physics = physics.reshape(air_state.shape)
    along_term = jnp.einsum("flyx,xz->flyz", air_state, along_mat, precision=high)
    across_term = jnp.einsum("yz,flzx->flyx", across_mat, air_state, precision=high)
    local_term = -viscosity * (
        weight_rows[:, None] * along_term + weight_cols[None, :] * across_term
    )
    mass = jacobian * (weight_rows[:, None] * weight_cols[None, :])
    stacked = jnp.concatenate(
        [local_term.reshape(2 * levels, row_count, col_count), mass[None]], axis=0
    )
    padded_cols = padded_2(stacked, (("fx", 2),), 1)
    along_sum = partner_sum(stacked, padded_cols, col_index, 2)
    padded_rows = padded_2(along_sum, (("fy", 1),), 1)
    summed = partner_sum(along_sum, padded_rows, row_index, 1)
    dynamics = (summed[:-1] / summed[-1]).reshape(air_state.shape)
    return air_state + 0.05 * dynamics + physics


def solution(mesh):
    placed = (P(None, None, "fy", "fx"), P("fy", "fx"), P("fy", "fx"), P(), P("fy", "fx"))
    return jax.shard_map(
        body, mesh=mesh, in_specs=placed, out_specs=P(None, None, "fy", "fx"), check_vma=False
    )
```

profile of v0, /device:TPU:11, one launch (start us, length us, event | category | flops | bytes accessed | tf_op | source)
XLA Modules:
  0.0 250.3 jit_solution(15425365600110330069)
XLA Ops:
  2.3 5.7 %all-to-all-start = ((s32[8,1,4]{2,1,0:T(1,128)}), s32[8,1,4]{2,1,0:T(1,128)S(1)}, u32[]{:S(2)}, u32[]{:S(2)}) async-start(s32[8,1,4]{2,1,0:T(1,128)} %bitcast.13), calls=%async_computation | async-start | bytes 8192 | tf_op jit(solution)/shard_map/all_to_all | solution.py:97
  12.6 3.5 %copy.72 = bf16[8,4,116,256]{3,1,2,0:T(4,128)(2,1)} copy(bf16[8,4,116,256]{3,1,0,2:T(4,128)(2,1)} %reshape.108) | data formatting | bytes 3801088 | tf_op jit(solution)/shard_map/reshape | solution.py:93
  16.1 5.4 %all-to-all-start.1 = ((bf16[8,4,116,256]{3,1,2,0:T(4,128)(2,1)}), bf16[8,4,116,256]{3,1,2,0:T(4,128)(2,1)S(1)}, u32[]{:S(2)}, u32[]{:S(2)}) async-start(bf16[8,4,116,256]{3,1,2,0:T(4,128)(2,1)} %copy.72), calls=%async_computation.1 | async-start | bytes 3801088 | tf_op jit(solution)/shard_map/all_to_all | solution.py:96
  23.1 40.0 %all-to-all-done.1 = bf16[8,4,116,256]{3,1,2,0:T(4,128)(2,1)S(1)} async-done(((bf16[8,4,116,256]{3,1,2,0:T(4,128)(2,1)}), bf16[8,4,116,256]{3,1,2,0:T(4,128)(2,1)S(1)}, u32[]{:S(2)}, u32[]{:S(2)}) %all-to-all-start.1) | async-done | bytes 1900576 | tf_op jit(solution)/shard_map/all_to_all | solution.py:96
  65.4 4.1 %reshape.109 = bf16[32,116,256]{2,0,1:T(8,128)(2,1)} reshape(bf16[8,4,116,256]{3,1,0,2:T(4,128)(2,1)} %copy.73) | data formatting | bytes 3801088 | tf_op jit(solution)/shard_map/reshape | solution.py:105
  71.8 34.4 %while.12 = (s32[]{:T(128)}, f32[8,58,256]{2,1,0:T(8,128)S(1)}, f32[8,58,256]{2,1,0:T(8,128)S(1)}, f32[58,58]{1,0:T(8,128)S(1)}, s32[]{:T(128)}) while((s32[]{:T(128)}, f32[8,58,256]{2,1,0:T(8,128)S(1)}, f32[8,58,256]{2,1,0:T(8,128)S(1)}, f32[58,58]{1,0:T(8,128)S(1)}, s32[]{:T(128)}) %tuple.32), condition=%wide.region_4.5_spmd, body=%wide.region_3.4_spmd.sunk | while | flops 85049344 | bytes 4764877 | solution.py:56
  106.7 3.6 %fusion.17 = f32[32,116,256]{2,0,1:T(8,128)} fusion(f32[8,58,256]{2,0,1:T(8,128)S(1)} %get-tuple-element.63, f32[8,58,256]{2,0,1:T(8,128)S(1)} %get-tuple-element.62, s32[32]{0:T(128)S(1)} %add_reduce_fusion, pred[32]{0:T(512)(128)(4,1)S(1)} %eq.94), kind=kOutput, calls=%fused_computation.35 | convolution fusion | flops 91464192 | bytes 4751520 | tf_op jit(solution)/shard_map/rs,rkx->skx/dot_general | solution.py:110
  110.3 5.1 %reshape.110 = f32[8,4,116,256]{3,1,0,2:T(4,128)} reshape(f32[32,116,256]{2,0,1:T(8,128)} %fusion.17) | data formatting | bytes 7602176 | tf_op jit(solution)/shard_map/reshape | solution.py:112
  115.4 4.6 %copy.78 = f32[8,4,116,256]{3,1,2,0:T(4,128)} copy(f32[8,4,116,256]{3,1,0,2:T(4,128)} %reshape.110) | data formatting | bytes 7602176 | tf_op jit(solution)/shard_map/reshape | solution.py:112
  120.0 6.5 %all-to-all-start.2 = ((f32[8,4,116,256]{3,1,2,0:T(4,128)}), f32[8,4,116,256]{3,1,2,0:T(4,128)}, u32[]{:S(2)}, u32[]{:S(2)}) async-start(f32[8,4,116,256]{3,1,2,0:T(4,128)} %copy.78), calls=%async_computation.2 | async-start | bytes 7602176 | tf_op jit(solution)/shard_map/all_to_all | solution.py:111
  126.7 5.7 %fusion.41 = f32[256,2,58,32]{0,3,2,1:T(8,128)S(1)} fusion(f32[256,256,1,1]{1,0,3,2:T(8,128)S(1)} %copy-done.4, f32[2,58,32,256]{3,2,1,0:T(8,128)} %param.11), kind=kOutput, calls=%fused_computation.72 | convolution fusion | flops 2919235584 | bytes 7864320 | tf_op jit(solution)/shard_map/flyx,xz->flyz/dot_general | solution.py:125
  132.4 4.1 %fusion.14 = f32[2,58,32,256]{3,2,1,0:T(8,128)S(1)} fusion(f32[256,2,58,32]{0,3,2,1:T(8,128)S(1)} %fusion.41, f32[32,32,1,1]{1,0,3,2:T(8,128)S(1)} %copy-done.7, f32[2,58,32,256]{3,2,1,0:T(8,128)S(1)} %copy-done, f32[256]{0:T(256)S(1)} %copy-done.8, f32[32]{0:T(128)S(1)} %copy-done.9, f32[32,256]{1,0:T(8,128)S(1)} %neg.7), kind=kOutput, calls=%fused_computation.28 | convolution fusion | flops 368705536 | bytes 11441280 | tf_op jit(solution)/shard_map/yz,flzx->flyx/dot_general | solution.py:126
  136.5 2.5 fusion.15
  139.0 2.6 %copy.65 = f32[117,32,1]{0,1,2:T(8,128)S(1)} copy(f32[117,32,1]{2,1,0:T(8,128)} %get-tuple-element.60) | data formatting | bytes 29952 | tf_op jit(solution)/shard_map/slice | solution.py:19
  145.4 63.4 %collective-permute-done = f32[117,32,1]{0,1,2:T(8,128)S(1)} collective-permute-done((f32[117,32,1]{0,1,2:T(8,128)S(1)}, f32[117,32,1]{0,1,2:T(8,128)S(1)}, u32[]{:S(2)}, u32[]{:S(2)}) %collective-permute-start) | collective-permute-done | bytes 15008 | tf_op jit(solution)/shard_map/ppermute | solution.py:19
  210.6 2.8 %copy.68 = f32[117,32,1]{2,1,0:T(8,128)} copy(f32[117,32,1]{0,1,2:T(8,128)S(1)} %collective-permute-done.1) | data formatting | bytes 29952 | tf_op jit(solution)/shard_map/ppermute | solution.py:16
  213.4 7.1 %fusion.7 = f32[117,32,256]{2,1,0:T(8,128)S(1)} fusion(f32[1,32,256]{2,1,0:T(8,128)S(1)} %multiply_bitcast_fusion, f32[117,32,1]{2,1,0:T(8,128)} %copy.68, f32[116,32,256]{2,1,0:T(8,128)} %bitcast.61, f32[117,32,1]{2,1,0:T(8,128)S(1)} %copy.66, pred[256]{0:T(512)(128)(4,1)S(1)} %get-tuple-element.66, pred[256]{0:T(512)(128)(4,1)S(1)} %get-tuple-element.67), kind=kLoop, calls=%fused_computation.13 | loop fusion | flops 7667712 | bytes 7698176 | tf_op jit(solution)/shard_map/add | solution.py:64
  220.7 2.8 %collective-permute-start.2 = (f32[117,1,256]{2,1,0:T(1,128)S(1)}, f32[117,1,256]{2,1,0:T(1,128)S(1)}, u32[]{:S(2)}, u32[]{:S(2)}) collective-permute-start(f32[117,1,256]{2,1,0:T(1,128)S(1)} %get-tuple-element.58), channel_id=1, source_target_pairs={{1,0},{2,1},{3,2},{0,3},{5,4},{6,5},{7,6},{4,7},{9,8},{10,9},{11,1... | collective-permute-start | bytes 359432 | tf_op jit(solution)/shard_map/ppermute | solution.py:19
  224.7 4.0 %collective-permute-done.2 = f32[117,1,256]{2,1,0:T(1,128)S(1)} collective-permute-done((f32[117,1,256]{2,1,0:T(1,128)S(1)}, f32[117,1,256]{2,1,0:T(1,128)S(1)}, u32[]{:S(2)}, u32[]{:S(2)}) %collective-permute-start.2) | collective-permute-done | bytes 119840 | tf_op jit(solution)/shard_map/ppermute | solution.py:19
  230.1 2.4 fusion.13
  232.5 5.1 %copy.79 = f32[8,4,116,256]{3,1,0,2:T(4,128)} copy(f32[8,4,116,256]{3,1,2,0:T(4,128)} %all-to-all-done.2) | data formatting | bytes 7602176 | tf_op jit(solution)/shard_map/all_to_all | solution.py:111
  237.6 5.1 %reshape.111 = f32[32,116,256]{2,0,1:T(8,128)} reshape(f32[8,4,116,256]{3,1,0,2:T(4,128)} %copy.79) | data formatting | bytes 7602176 | tf_op jit(solution)/shard_map/reshape | solution.py:121
  242.7 4.2 %fusion.23 = f32[116,256,32]{1,2,0:T(8,128)S(1)} fusion(f32[32,116,256]{2,0,1:T(8,128)} %reshape.111, s32[32]{0:T(128)S(1)} %compare_select_fusion.2), kind=kOutput, calls=%fused_computation.49 | convolution fusion | flops 364905472 | bytes 7602304 | tf_op jit(solution)/shard_map/sb,skx->kbx/dot_general | solution.py:118
  247.1 3.2 %add_add_fusion = f32[2,58,32,256]{3,2,1,0:T(8,128)} fusion(f32[2,58,32,256]{3,2,1,0:T(8,128)S(1)} %bitcast.63, f32[2,58,32,256]{3,2,1,0:T(8,128)S(1)} %copy-done.1, f32[2,58,32,256]{3,2,1,0:T(8,128)S(1)} %bitcast.62), kind=kLoop, calls=%fused_computation.29 | loop fusion | flops 1900544 | bytes 15204352 | tf_op jit(solution)/shard_map/add | solution.py:139
  (155 shorter events, 55.7 us)
Async XLA Ops:
  2.3 13.8 %all-to-all-start = ((s32[8,1,4]{2,1,0:T(1,128)}), s32[8,1,4]{2,1,0:T(1,128)S(1)}, u32[]{:S(2)}, u32[]{:S(2)}) async-start(s32[8,1,4]{2,1,0:T(1,128)} %bitcast.13), calls=%async_computation | async-start | bytes 8192 | tf_op jit(solution)/shard_map/all_to_all | solution.py:97
  16.1 46.9 %all-to-all-start.1 = ((bf16[8,4,116,256]{3,1,2,0:T(4,128)(2,1)}), bf16[8,4,116,256]{3,1,2,0:T(4,128)(2,1)S(1)}, u32[]{:S(2)}, u32[]{:S(2)}) async-start(bf16[8,4,116,256]{3,1,2,0:T(4,128)(2,1)} %copy.72), calls=%async_computation.1 | async-start | bytes 3801088 | tf_op jit(solution)/shard_map/all_to_all | solution.py:96
  69.5 2.3 copy-start.10
  120.0 6.5 %copy-start.5 = (f32[32,256]{1,0:T(8,128)S(1)}, f32[32,256]{1,0:T(8,128)}, u32[]{:S(2)}) copy-start(f32[32,256]{1,0:T(8,128)} %param.13) | copy-start | bytes 98308
  120.0 6.5 %copy-start.6 = (f32[32,256]{1,0:T(8,128)S(1)}, f32[32,256]{1,0:T(8,128)}, u32[]{:S(2)}) copy-start(f32[32,256]{1,0:T(8,128)} %param.12) | copy-start | bytes 98308
  120.0 6.5 %copy-start.8 = (f32[256]{0:T(256)S(1)}, f32[256]{0:T(256)}, u32[]{:S(2)}) copy-start(f32[256]{0:T(256)} %constant.69.clone) | copy-start | bytes 3076
  120.0 6.6 %copy-start.9 = (f32[32]{0:T(128)S(1)}, f32[32]{0:T(128)}, u32[]{:S(2)}) copy-start(f32[32]{0:T(128)} %constant.68.clone) | copy-start | bytes 388
  120.0 6.6 %copy-start.4 = (f32[256,256,1,1]{1,0,3,2:T(8,128)S(1)}, f32[256,256,1,1]{1,0,3,2:T(8,128)}, u32[]{:S(2)}) copy-start(f32[256,256,1,1]{1,0,3,2:T(8,128)} %constant.71) | copy-start | bytes 786436
  120.0 112.5 %all-to-all-start.2 = ((f32[8,4,116,256]{3,1,2,0:T(4,128)}), f32[8,4,116,256]{3,1,2,0:T(4,128)}, u32[]{:S(2)}, u32[]{:S(2)}) async-start(f32[8,4,116,256]{3,1,2,0:T(4,128)} %copy.78), calls=%async_computation.2 | async-start | bytes 7602176 | tf_op jit(solution)/shard_map/all_to_all | solution.py:111
  126.7 5.7 %copy-start = (f32[2,58,32,256]{3,2,1,0:T(8,128)S(1)}, f32[2,58,32,256]{3,2,1,0:T(8,128)}, u32[]{:S(2)}) copy-start(f32[2,58,32,256]{3,2,1,0:T(8,128)} %param.11) | copy-start | bytes 11403268
  126.7 5.7 %copy-start.7 = (f32[32,32,1,1]{1,0,3,2:T(8,128)S(1)}, f32[32,32,1,1]{1,0,3,2:T(8,128)}, u32[]{:S(2)}) copy-start(f32[32,32,1,1]{1,0,3,2:T(8,128)} %constant.72) | copy-start | bytes 12292
  136.5 2.5 copy-start.2
  141.5 67.3 %collective-permute-start = (f32[117,32,1]{0,1,2:T(8,128)S(1)}, f32[117,32,1]{0,1,2:T(8,128)S(1)}, u32[]{:S(2)}, u32[]{:S(2)}) collective-permute-start(f32[117,32,1]{0,1,2:T(8,128)S(1)} %copy.65), channel_id=1, source_target_pairs={{4,0},{8,4},{12,8},{16,12},{20,16},{24,20},{28,24},{0,28},{5,1},{9... | collective-permute-start | bytes 44936 | tf_op jit(solution)/shard_map/ppermute | solution.py:19
  143.1 67.5 %collective-permute-start.1 = (f32[117,32,1]{0,1,2:T(8,128)S(1)}, f32[117,32,1]{0,1,2:T(8,128)S(1)}, u32[]{:S(2)}, u32[]{:S(2)}) collective-permute-start(f32[117,32,1]{0,1,2:T(8,128)S(1)} %copy.67), channel_id=1, source_target_pairs={{0,4},{4,8},{8,12},{12,16},{16,20},{20,24},{24,28},{28,0},{1,5},{5... | collective-permute-start | bytes 44936 | tf_op jit(solution)/shard_map/ppermute | solution.py:16
  220.7 8.0 %collective-permute-start.2 = (f32[117,1,256]{2,1,0:T(1,128)S(1)}, f32[117,1,256]{2,1,0:T(1,128)S(1)}, u32[]{:S(2)}, u32[]{:S(2)}) collective-permute-start(f32[117,1,256]{2,1,0:T(1,128)S(1)} %get-tuple-element.58), channel_id=1, source_target_pairs={{1,0},{2,1},{3,2},{0,3},{5,4},{6,5},{7,6},{4,7},{9,8},{10,9},{11,1... | collective-permute-start | bytes 359432 | tf_op jit(solution)/shard_map/ppermute | solution.py:19
  223.5 5.2 %collective-permute-start.3 = (f32[117,1,256]{2,1,0:T(1,128)S(1)}, f32[117,1,256]{2,1,0:T(1,128)S(1)}, u32[]{:S(2)}, u32[]{:S(2)}) collective-permute-start(f32[117,1,256]{2,1,0:T(1,128)S(1)} %get-tuple-element.59), channel_id=1, source_target_pairs={{0,1},{1,2},{2,3},{3,0},{4,5},{5,6},{6,7},{7,4},{8,9},{9,10},{10,1... | collective-permute-start | bytes 359432 | tf_op jit(solution)/shard_map/ppermute | solution.py:16
  242.7 4.2 %copy-start.1 = (f32[2,58,32,256]{3,2,1,0:T(8,128)S(1)}, f32[2,58,32,256]{3,2,1,0:T(8,128)}, u32[]{:S(2)}) copy-start(f32[2,58,32,256]{3,2,1,0:T(8,128)} %param.11) | copy-start | bytes 11403268
  242.7 4.4 %copy-start.3 = (f32[116,32,256]{2,1,0:T(8,128)S(1)}, f32[116,32,256]{2,1,0:T(8,128)}, u32[]{:S(2)}) copy-start(f32[116,32,256]{2,1,0:T(8,128)} %fusion.13) | copy-start | bytes 11403268
where the time goes:
time: 251 us; the launch traced here: 250 us
  waiting for transfers between devices  107 us (43%)
  local copies, waits for them, and re-layouts  43.5 us (17%)
  matrix products  43.3 us (17%)
  other arithmetic  30.5 us (12%)
  starting transfers between devices  24.2 us (10%)
    ppermute x2, waiting for transfers between devices, padded_2(): lax.ppermute(lax.slice_in_dim(block, 0, width, axis=dim), axis, backward)  67.5 us
    all_to_all x1, waiting for transfers between devices, body(): lax.all_to_all(packed, 'fx', split_axis=0, concat_axis=0, tiled=True)  40 us
    dot_general x24, matrix products, substep(): jnp.einsum(pattern, mixing, cond, precision=lax.Precision.HIGHEST)  23.2 us
    reshape x2, local copies, waits for them, and re-layouts, body(): back_slots.reshape(slab_count, cap, 2 * levels, col_count)  9.7 us
    add x2, other arithmetic, partner_sum(): values + jnp.where(index_vec == 3, upper, jnp.where(index_vec == 0, lower...  8.55 us
    sub x24, other arithmetic, substep(): moist_now = moist_now - 0.25 * cond  8.4 us
    all_to_all x1, starting transfers between devices, body(): lax.all_to_all(back_slots.reshape(slab_count, cap, 2 * levels, col_count)...  6.51 us
    dot_general x1, matrix products, body(): jnp.einsum('flyx,xz->flyz', air_state, along_mat, precision=high)  5.71 us
  transfers between devices with their start and end apart: 7, of which 3 were waited for; matrix products, arithmetic and copies ran while one was open for 17% of the time, Pallas kernels for 0%

commit v1 on v0

v1 whole, which is shorter than its diff:
```python
import jax
import jax.numpy as jnp
import numpy as np
from jax import lax
from jax.experimental import pallas as pl
from jax.experimental.pallas import tpu as pltpu
from jax.sharding import PartitionSpec as P

SUBSTEPS = 24
LOG2E = float(np.log2(np.e))
LN2 = float(np.log(2.0))
LANES = 128
TILE = 8
F32 = jnp.float32
BF16 = jnp.bfloat16


def gll_tables():
    nodes = np.array([-1.0, -1.0 / np.sqrt(5.0), 1.0 / np.sqrt(5.0), 1.0])
    gll_weight = np.array([1.0 / 6.0, 5.0 / 6.0, 5.0 / 6.0, 1.0 / 6.0])
    deriv = np.zeros((4, 4))
    for first in range(4):
        for second in range(4):
            if first == second:
                deriv[first, second] = sum(
                    (1.0 / (nodes[first] - nodes[other]) for other in range(4) if other != first)
                )
            else:
                top = np.prod([nodes[first] - nodes[other] for other in range(4) if other != first])
                below = np.prod(
                    [nodes[second] - nodes[other] for other in range(4) if other != second]
                )
                deriv[first, second] = top / below / (nodes[first] - nodes[second])
    stiff = deriv.T * gll_weight[None, :] @ deriv
    return (stiff, gll_weight)


def by_node(index, values):
    node = index % 4
    result = jnp.full(index.shape, values[0], F32)
    for k in range(1, 4):
        result = jnp.where(node == k, F32(values[k]), result)
    return result


def split(value):
    high = value.astype(BF16)
    low = (value - high.astype(F32)).astype(BF16)
    return high, low


def sum_cols(g):
    n = g.shape[-1]
    col = lax.broadcasted_iota(jnp.int32, g.shape, 1)
    upper = pltpu.roll(g, n - 1, 1)
    lower = pltpu.roll(g, 1, 1)
    up = (col % 4 == 3) & (col != n - 1)
    low = (col % 4 == 0) & (col != 0)
    return g + jnp.where(up, upper, jnp.where(low, lower, 0.0))


def sum_rows(g, first=0.0, last=0.0):
    n = g.shape[0]
    row = lax.broadcasted_iota(jnp.int32, g.shape, 0)
    upper = jnp.where(row == n - 1, last, pltpu.roll(g, n - 1, 0))
    lower = jnp.where(row == 0, first, pltpu.roll(g, 1, 0))
    return g + jnp.where(row % 4 == 3, upper, jnp.where(row % 4 == 0, lower, 0.0))


def local_kernel(
    air, jac, visc, khi, klo, summed, msum, col_lo, col_hi, row_lo, row_hi, along, fa, fb
):
    step = pl.program_id(0)
    chunk, rows, cols = air.shape
    stiff, weight = gll_tables()

    @pl.when(step == 0)
    def _():
        r = lax.broadcasted_iota(jnp.int32, (rows, cols), 0)
        c = lax.broadcasted_iota(jnp.int32, (rows, cols), 1)
        wr, wc = by_node(r, weight), by_node(c, weight)
        fa[...] = -visc[...] * wr
        fb[...] = -visc[...] * wc
        mass = jac[...] * (wr * wc)
        msum[...] = sum_rows(sum_cols(mass))
        slot = pl.num_programs(0) * chunk
        lane = lax.broadcasted_iota(jnp.int32, (rows, LANES), 1)
        col_lo[...] = jnp.where(lane == slot, pltpu.roll(mass[:, :LANES], slot % LANES, 1), 0.0)
        col_hi[...] = jnp.where(
            lane == slot, pltpu.roll(mass[:, cols - LANES :], (slot + 1) % LANES, 1), 0.0
        )
        row_lo[...] = jnp.zeros_like(row_lo)
        row_hi[...] = jnp.zeros_like(row_hi)
        row_lo[pl.ds(slot, 1), :] = mass[0:1, :]
        row_hi[pl.ds(slot, 1), :] = mass[rows - 1 :, :]

    high, low = split(air[...].reshape(chunk * rows, cols))
    along[...] = (
        jnp.dot(high, khi[...], preferred_element_type=F32)
        + jnp.dot(low, khi[...], preferred_element_type=F32)
        + jnp.dot(high, klo[...], preferred_element_type=F32)
    ).reshape(chunk, rows, cols)

    sub = lax.broadcasted_iota(jnp.int32, (TILE, cols), 0)
    coefs = []
    for d in range(-3, 4):
        values = [stiff[k, k + d] if 0 <= k + d < 4 else 0.0 for k in range(4)]
        coefs.append((d, by_node(sub, values)))

    def level(i, _):
        index = step * chunk + i
        f = air[i].reshape(rows // TILE, TILE, cols)
        across = jnp.zeros_like(f)
        for d, coef in coefs:
            moved = f if d == 0 else pltpu.roll(f, (-d) % TILE, 1)
            across = across + coef[None] * moved
        local = fa[...] * along[i] + fb[...] * across.reshape(rows, cols)
        lane = lax.broadcasted_iota(jnp.int32, (rows, LANES), 1)
        mine = lane == index
        col_lo[...] = jnp.where(mine, pltpu.roll(local[:, :LANES], index, 1), col_lo[...])
        col_hi[...] = jnp.where(
            mine, pltpu.roll(local[:, cols - LANES :], index + 1, 1), col_hi[...]
        )
        row_lo[pl.ds(index, 1), :] = local[0:1, :]
        row_hi[pl.ds(index, 1), :] = local[rows - 1 :, :]
        summed[i] = sum_rows(sum_cols(local))
        return 0

    lax.fori_loop(0, chunk, level, 0, unroll=2 if chunk % 2 == 0 else 1)


def softplus2(y):
    return jnp.maximum(y, 0.0) + jnp.log2(1.0 + jnp.exp2(-jnp.abs(y)))


def physics_kernel(flag, mixing, air, out, y, csum):
    levels, rows, cols = air.shape[1:]
    depth = y.shape[1]

    @pl.when(flag[0] > 0)
    def _():
        t = air[0].astype(BF16).astype(F32)
        q = air[1].astype(BF16).astype(F32)
        x = (q - 0.5 * t) * LOG2E
        y[...] = jnp.zeros_like(y)
        csum[...] = jnp.zeros_like(csum)
        for r in range(rows):
            y[r, :levels, :] = x[:, r, :]
        eye = lax.broadcasted_iota(jnp.int32, (depth, depth), 0) == lax.broadcasted_iota(
            jnp.int32, (depth, depth), 1
        )
        mix = mixing[...]
        ahigh, alow = split(0.125 * mix + jnp.where(eye, 0.25, 0.0))
        acat = jnp.concatenate([ahigh, ahigh, alow], axis=1)

        def substep(_, carry):
            for r in range(rows):
                value = y[r]
                cond = softplus2(value)
                csum[r] += cond
                high, low = split(cond)
                stack = jnp.concatenate([high, low, high], axis=0)
                y[r] = value - jnp.dot(acat, stack, preferred_element_type=F32)
            return carry

        lax.fori_loop(0, SUBSTEPS, substep, 0)
        mhigh, mlow = split(0.25 * mix)
        mcat = jnp.concatenate([mhigh, mhigh, mlow], axis=1)
        for r in range(rows):
            total = csum[r] * LN2
            high, low = split(total)
            stack = jnp.concatenate([high, low, high], axis=0)
            heat = jnp.dot(mcat, stack, preferred_element_type=F32)
            out[0, :, r, :] = heat[:levels]
            out[1, :, r, :] = -0.25 * total[:levels]


def final_kernel(
    flag, air, summed, phys, msum, left, right, below, above, lb, la, rb, ra, out,
    inv, edge_l, edge_r, edge_b, edge_a,
):
    step = pl.program_id(0)
    chunk, rows, cols = air.shape
    row = lax.broadcasted_iota(jnp.int32, (rows, cols), 0)
    col = lax.broadcasted_iota(jnp.int32, (rows, cols), 1)

    def full(base, index):
        west = pltpu.roll(edge_l[...], (LANES - index) % LANES, 1)
        east = pltpu.roll(edge_r[...], (2 * LANES - 1 - index) % LANES, 1)
        zero = jnp.zeros((rows, cols - LANES), F32)
        base = base + jnp.where(col == 0, jnp.concatenate([west, zero], axis=1), 0.0)
        base = base + jnp.where(col == cols - 1, jnp.concatenate([zero, east], axis=1), 0.0)
        base = base + jnp.where(row == 0, edge_b[pl.ds(index, 1), :], 0.0)
        return base + jnp.where(row == rows - 1, edge_a[pl.ds(index, 1), :], 0.0)

    @pl.when(step == 0)
    def _():
        edge_l[...] = sum_rows(left[...], lb[...], la[...])
        edge_r[...] = sum_rows(right[...], rb[...], ra[...])
        edge_b[...] = sum_cols(below[...])
        edge_a[...] = sum_cols(above[...])
        inv[...] = 0.05 / full(msum[...], pl.num_programs(0) * chunk)

    def levels_with(extra):
        def level(i, _):
            total = full(summed[i], step * chunk + i)
            value = air[i] + inv[...] * total
            if extra:
                value = value + phys[i]
            out[i] = value
            return 0

        lax.fori_loop(0, chunk, level, 0)

    @pl.when(flag[0] > 0)
    def _():
        levels_with(True)

    @pl.when(flag[0] <= 0)
    def _():
        levels_with(False)


def body(air_state, jacobian, viscosity, mixing, convect_dest):
    _, levels, rows, cols = air_state.shape
    planes = 2 * levels
    chunk = levels // 2
    steps = planes // chunk
    flat = air_state.reshape(planes, rows, cols)
    stiff, _ = gll_tables()
    along_mat = np.kron(np.eye(cols // 4), stiff).astype(np.float32)
    khi = along_mat.astype(jnp.bfloat16)
    klo = (along_mat - khi.astype(np.float32)).astype(jnp.bfloat16)
    row_slots = -(-(planes + 1) // TILE) * TILE
    flag = (convect_dest[:1, 0] >= 0).astype(jnp.int32)

    def whole(shape):
        return pl.BlockSpec(shape, lambda *_: (0,) * len(shape))

    plane_spec = pl.BlockSpec((chunk, rows, cols), lambda i, *_: (i, 0, 0))
    plane = jax.ShapeDtypeStruct((planes, rows, cols), F32)
    edge_col = jax.ShapeDtypeStruct((rows, LANES), F32)
    edge_row = jax.ShapeDtypeStruct((row_slots, cols), F32)
    summed, msum, col_lo, col_hi, row_lo, row_hi = pl.pallas_call(
        local_kernel,
        grid=(steps,),
        out_shape=[
            plane, jax.ShapeDtypeStruct((rows, cols), F32), edge_col, edge_col, edge_row, edge_row,
        ],
        in_specs=[plane_spec] + [whole((rows, cols))] * 2 + [whole((cols, cols))] * 2,
        out_specs=[
            plane_spec, whole((rows, cols)), whole((rows, LANES)), whole((rows, LANES)),
            whole((row_slots, cols)), whole((row_slots, cols)),
        ],
        scratch_shapes=[
            pltpu.VMEM((chunk, rows, cols), F32),
            pltpu.VMEM((rows, cols), F32),
            pltpu.VMEM((rows, cols), F32),
        ],
        compiler_params=pltpu.CompilerParams(vmem_limit_bytes=32 * 2**20),
        name="local_terms",
    )(flat, jacobian, viscosity, khi, klo)

    nx, ny = lax.axis_size("fx"), lax.axis_size("fy")

    def shifted(value, dx, dy):
        if dy == 0:
            pairs = [((i + dx) % nx, i) for i in range(nx)]
            return lax.ppermute(value, "fx", pairs)
        if dx == 0:
            pairs = [((j + dy) % ny, j) for j in range(ny)]
            return lax.ppermute(value, "fy", pairs)
        pairs = [
            (((i + dx) % nx) * ny + (j + dy) % ny, i * ny + j) for i in range(nx) for j in range(ny)
        ]
        return lax.ppermute(value, ("fx", "fy"), pairs)

    left, right = shifted(col_hi, -1, 0), shifted(col_lo, 1, 0)
    below, above = shifted(row_hi, 0, -1), shifted(row_lo, 0, 1)
    lb, la = shifted(col_hi[rows - 1 :], -1, -1), shifted(col_hi[:1], -1, 1)
    rb, ra = shifted(col_lo[rows - 1 :], 1, -1), shifted(col_lo[:1], 1, 1)

    depth = -(-levels // 16) * 16
    mix = jnp.zeros((depth, depth), F32).at[:levels, :levels].set(mixing)
    group = TILE
    air_spec = pl.BlockSpec(
        (2, levels, group, cols), lambda i, flag: (0, 0, i * flag[0], 0)
    )
    phys = pl.pallas_call(
        physics_kernel,
        grid_spec=pltpu.PrefetchScalarGridSpec(
            num_scalar_prefetch=1,
            grid=(rows // group,),
            in_specs=[whole((depth, depth)), air_spec],
            out_specs=air_spec,
            scratch_shapes=[pltpu.VMEM((group, depth, cols), F32)] * 2,
        ),
        out_shape=jax.ShapeDtypeStruct(air_state.shape, F32),
        compiler_params=pltpu.CompilerParams(vmem_limit_bytes=32 * 2**20),
        cost_estimate=pl.CostEstimate(
            flops=2 * SUBSTEPS * rows * cols * depth * depth * 6,
            bytes_accessed=16 * levels * rows * cols,
            transcendentals=2 * SUBSTEPS * rows * cols * depth,
        ),
        name="column_physics",
    )(flag, mix, air_state)

    phys_spec = pl.BlockSpec((chunk, rows, cols), lambda i, flag: (i * flag[0], 0, 0))
    result = pl.pallas_call(
        final_kernel,
        grid_spec=pltpu.PrefetchScalarGridSpec(
            num_scalar_prefetch=1,
            grid=(steps,),
            in_specs=[
                plane_spec, plane_spec, phys_spec, whole((rows, cols)),
                whole((rows, LANES)), whole((rows, LANES)),
                whole((row_slots, cols)), whole((row_slots, cols)),
            ] + [whole((1, LANES))] * 4,
            out_specs=plane_spec,
            scratch_shapes=[
                pltpu.VMEM((rows, cols), F32),
                pltpu.VMEM((rows, LANES), F32),
                pltpu.VMEM((rows, LANES), F32),
                pltpu.VMEM((row_slots, cols), F32),
                pltpu.VMEM((row_slots, cols), F32),
            ],
        ),
        out_shape=plane,
        compiler_params=pltpu.CompilerParams(vmem_limit_bytes=32 * 2**20),
        name="step_sum",
    )(flag, flat, summed, phys.reshape(planes, rows, cols), msum, left, right, below, above,
      lb, la, rb, ra)
    return result.reshape(air_state.shape)


def solution(mesh):
    placed = (P(None, None, "fy", "fx"), P("fy", "fx"), P("fy", "fx"), P(), P("fy", "fx"))
    return jax.shard_map(
        body, mesh=mesh, in_specs=placed, out_specs=P(None, None, "fy", "fx"), check_vma=False
    )
```

time: 251 us -> 87.4 us (0.35)
  the two profiles are of different devices: /device:TPU:11 before, /device:TPU:8 now
where the time goes in v1:
time: 87.4 us; the launch traced here: 86.4 us
  Pallas kernels  68.3 us (78%)
  starting transfers between devices  9.68 us (11%)
  local copies, waits for them, and re-layouts  5.43 us (6%)
  waiting for transfers between devices  2.8 us (3%)
    pallas_call x1, Pallas kernels, body(): pl.pallas_call(physics_kernel, grid_spec=pltpu.PrefetchScalarGridSpec(num...  41.7 us
    pallas_call x1, Pallas kernels, body(): pl.pallas_call(local_kernel, grid=(steps,), out_shape=[plane, jax.ShapeDt...  15.3 us
    pallas_call x1, Pallas kernels, body(): pl.pallas_call(final_kernel, grid_spec=pltpu.PrefetchScalarGridSpec(num_s...  11.2 us
    ppermute x4, starting transfers between devices, shifted(): return lax.ppermute(value, ('fx', 'fy'), pairs)  5.46 us
    unnamed x14, local copies, waits for them, and re-layouts  5.42 us
    ppermute x4, waiting for transfers between devices, shifted(): return lax.ppermute(value, ('fx', 'fy'), pairs)  2.79 us
    ppermute x2, starting transfers between devices, shifted(): return lax.ppermute(value, 'fy', pairs)  2.79 us
  transfers between devices with their start and end apart: 8, of which 2 were waited for; matrix products, arithmetic and copies ran while one was open for 0% of the time, Pallas kernels for 48%

profile of v1, /device:TPU:8, one launch (start us, length us, event | category | flops | bytes accessed | tf_op | source)
XLA Modules:
  0.0 86.4 jit_solution(6151762863243950357)
XLA Ops:
  0.0 2.1 %copy-done = f32[2,58,32,256]{3,2,1,0:T(8,128)S(1)} copy-done((f32[2,58,32,256]{3,2,1,0:T(8,128)S(1)}, f32[2,58,32,256]{3,2,1,0:T(8,128)}, u32[]{:S(2)}) %copy-start) | copy-done | bytes 3801112
  2.1 0.9 %copy-done.1 = bf16[256,256]{1,0:T(8,128)(2,1)S(1)} copy-done((bf16[256,256]{1,0:T(8,128)(2,1)S(1)}, bf16[256,256]{1,0:T(8,128)(2,1)}, u32[]{:S(2)}) %copy-start.1) | copy-done | bytes 131096
  3.0 0.9 %copy-done.2 = bf16[256,256]{1,0:T(8,128)(2,1)S(1)} copy-done((bf16[256,256]{1,0:T(8,128)(2,1)S(1)}, bf16[256,256]{1,0:T(8,128)(2,1)}, u32[]{:S(2)}) %copy-start.2) | copy-done | bytes 131096
  3.9 0.8 copy-done.3
  4.7 0.8 copy-done.4
  5.4 15.3 %local_terms.1 = (f32[116,32,256]{2,1,0:T(8,128)S(1)}, f32[32,256]{1,0:T(8,128)S(1)}, f32[32,128]{1,0:T(8,128)S(1)}, f32[32,128]{1,0:T(8,128)S(1)}, f32[120,256]{1,0:T(8,128)S(1)}, /*index=5*/f32[120,256]{1,0:T(8,128)S(1)}) custom-call(f32[116,32,256]{2,1,0:T(8,128)S(1)} %bitcast.5, f32[32,256]{1,0:T(8,128)S(1)} %copy-done.3, f32[32,256]{1,0:T(8,128)S(1)} %copy-done.4, ...), custom_call_target="tpu_custom_call" | custom-call | tf_op jit(solution)/shard_map/local_terms/pallas_call | solution.py:244
  20.8 1.4 %collective-permute-start.1 = (f32[32,128]{1,0:T(8,128)S(1)}, f32[32,128]{1,0:T(8,128)S(1)}, u32[]{:S(2)}, u32[]{:S(2)}) collective-permute-start(f32[32,128]{1,0:T(8,128)S(1)} %get-tuple-element.26), channel_id=1, source_target_pairs={{4,0},{8,4},{12,8},{16,12},{20,16},{24,20},{28,24},{0,28},{5,1},{9... | collective-permute-start | bytes 49160 | tf_op jit(solution)/shard_map/ppermute | solution.py:269
  22.2 0.7 collective-permute-start.7
  22.9 4.1 %collective-permute-start.6 = (f32[1,128]{1,0:T(1,128)S(1)}, f32[1,128]{1,0:T(1,128)S(1)}, u32[]{:S(2)}, u32[]{:S(2)}) collective-permute-start(f32[1,128]{1,0:T(1,128)S(1)} %get-tuple-element.30), channel_id=1, source_target_pairs={{7,0},{4,1},{5,2},{6,3},{11,4},{8,5},{9,6},{10,7},{15,8},{12,9},{1... | collective-permute-start | bytes 1544 | tf_op jit(solution)/shard_map/ppermute | solution.py:276
  27.0 0.0 collective-permute-start
  27.0 0.6 collective-permute-start.5
  27.7 0.0 collective-permute-done.7.ra
  27.7 0.1 collective-permute-start.4
  27.8 0.5 collective-permute-done.6.rb
  28.3 0.5 collective-permute-start.2
  28.8 2.3 %collective-permute-done.5.la = f32[1,128]{1,0:T(1,128)S(1)} collective-permute-done((f32[1,128]{1,0:T(1,128)S(1)}, f32[1,128]{1,0:T(1,128)S(1)}, u32[]{:S(2)}, u32[]{:S(2)}) %collective-permute-start.5) | collective-permute-done | bytes 544 | tf_op jit(solution)/shard_map/ppermute | solution.py:276
  31.1 2.3 %collective-permute-start.3 = (f32[120,256]{1,0:T(8,128)S(1)}, f32[120,256]{1,0:T(8,128)S(1)}, u32[]{:S(2)}, u32[]{:S(2)}) collective-permute-start(f32[120,256]{1,0:T(8,128)S(1)} %get-tuple-element.28), channel_id=1, source_target_pairs={{1,0},{2,1},{3,2},{0,3},{5,4},{6,5},{7,6},{4,7},{9,8},{10,9},{11,1... | collective-permute-start | bytes 368648 | tf_op jit(solution)/shard_map/ppermute | solution.py:272
  33.3 41.7 %column_physics.1 = f32[2,58,32,256]{3,2,1,0:T(8,128)S(1)} custom-call(s32[1]{0:T(128)} %bitcast.flag, f32[64,64]{1,0:T(8,128)S(1)} %scatter.4.mixing, f32[2,58,32,256]{3,2,1,0:T(8,128)S(1)} %copy-done), custom_call_target="tpu_custom_call" | custom-call | flops 9663676416 | bytes 7602176 | tf_op jit(solution)/shard_map/column_physics/pallas_call | solution.py:289
  75.1 0.0 collective-permute-done.4.lb
  75.1 0.0 collective-permute-done.left
  75.1 0.0 collective-permute-done.1.right
  75.1 0.0 collective-permute-done.2.below
  75.1 0.0 collective-permute-done.3.above
  75.1 11.2 %step_sum.1 = f32[116,32,256]{2,1,0:T(8,128)} custom-call(s32[1]{0:T(128)} %bitcast.flag, f32[116,32,256]{2,1,0:T(8,128)S(1)} %bitcast.6, f32[116,32,256]{2,1,0:T(8,128)S(1)} %get-tuple-element.23.summed, f32[116,32,256]{2,1,0:T(8,128)S(1)} %bitcast.7, f32[32,256]{1,0:T(8,128)S(1)} %get-tuple-element.24.msum, f32[32,128]{1,0:T(8,128)S(1)} %collective-permute-done.left, ...), custom_call_target="tpu_custom_call" | custom-call | tf_op jit(solution)/shard_map/step_sum/pallas_call | solution.py:309
  (12 shorter events, 0.0 us)
Async XLA Ops:
  0.0 27.6 %copy-start.6 = (s32[32,1]{0,1:T(1,128)S(1)}, s32[32,1]{0,1:T(1,128)}, u32[]{:S(2)}) copy-start(s32[32,1]{0,1:T(1,128)} %param.13) | copy-start | bytes 388
  0.0 2.1 %copy-start = (f32[2,58,32,256]{3,2,1,0:T(8,128)S(1)}, f32[2,58,32,256]{3,2,1,0:T(8,128)}, u32[]{:S(2)}) copy-start(f32[2,58,32,256]{3,2,1,0:T(8,128)} %air.1) | copy-start | bytes 11403268
  2.1 0.9 %copy-start.1 = (bf16[256,256]{1,0:T(8,128)(2,1)S(1)}, bf16[256,256]{1,0:T(8,128)(2,1)}, u32[]{:S(2)}) copy-start(bf16[256,256]{1,0:T(8,128)(2,1)} %constant.36.clone.klo) | copy-start | bytes 393220
  3.0 0.9 %copy-start.2 = (bf16[256,256]{1,0:T(8,128)(2,1)S(1)}, bf16[256,256]{1,0:T(8,128)(2,1)}, u32[]{:S(2)}) copy-start(bf16[256,256]{1,0:T(8,128)(2,1)} %constant.35.clone.khi) | copy-start | bytes 393220
  3.9 0.8 copy-start.3
  4.7 0.8 copy-start.4
  5.4 22.2 %copy-start.5 = (f32[58,58]{1,0:T(8,128)S(1)}, f32[58,58]{1,0:T(8,128)}, u32[]{:S(2)}) copy-start(f32[58,58]{1,0:T(8,128)} %param.12) | copy-start | bytes 40372
  20.8 54.3 %collective-permute-start.1 = (f32[32,128]{1,0:T(8,128)S(1)}, f32[32,128]{1,0:T(8,128)S(1)}, u32[]{:S(2)}, u32[]{:S(2)}) collective-permute-start(f32[32,128]{1,0:T(8,128)S(1)} %get-tuple-element.26), channel_id=1, source_target_pairs={{4,0},{8,4},{12,8},{16,12},{20,16},{24,20},{28,24},{0,28},{5,1},{9... | collective-permute-start | bytes 49160 | tf_op jit(solution)/shard_map/ppermute | solution.py:269
  22.2 5.5 %collective-permute-start.7 = (f32[1,128]{1,0:T(1,128)S(1)}, f32[1,128]{1,0:T(1,128)S(1)}, u32[]{:S(2)}, u32[]{:S(2)}) collective-permute-start(f32[1,128]{1,0:T(1,128)S(1)} %get-tuple-element.29), channel_id=1, source_target_pairs={{5,0},{6,1},{7,2},{4,3},{9,4},{10,5},{11,6},{8,7},{13,8},{14,9},{1... | collective-permute-start | bytes 1544 | tf_op jit(solution)/shard_map/ppermute | solution.py:276
  22.9 5.4 %collective-permute-start.6 = (f32[1,128]{1,0:T(1,128)S(1)}, f32[1,128]{1,0:T(1,128)S(1)}, u32[]{:S(2)}, u32[]{:S(2)}) collective-permute-start(f32[1,128]{1,0:T(1,128)S(1)} %get-tuple-element.30), channel_id=1, source_target_pairs={{7,0},{4,1},{5,2},{6,3},{11,4},{8,5},{9,6},{10,7},{15,8},{12,9},{1... | collective-permute-start | bytes 1544 | tf_op jit(solution)/shard_map/ppermute | solution.py:276
  27.0 48.1 %collective-permute-start = (f32[32,128]{1,0:T(8,128)S(1)}, f32[32,128]{1,0:T(8,128)S(1)}, u32[]{:S(2)}, u32[]{:S(2)}) collective-permute-start(f32[32,128]{1,0:T(8,128)S(1)} %get-tuple-element.25), channel_id=1, source_target_pairs={{28,0},{0,4},{4,8},{8,12},{12,16},{16,20},{20,24},{24,28},{29,1},{... | collective-permute-start | bytes 49160 | tf_op jit(solution)/shard_map/ppermute | solution.py:269
  27.0 4.1 %collective-permute-start.5 = (f32[1,128]{1,0:T(1,128)S(1)}, f32[1,128]{1,0:T(1,128)S(1)}, u32[]{:S(2)}, u32[]{:S(2)}) collective-permute-start(f32[1,128]{1,0:T(1,128)S(1)} %get-tuple-element.31), channel_id=1, source_target_pairs={{29,0},{30,1},{31,2},{28,3},{1,4},{2,5},{3,6},{0,7},{5,8},{6,9},{7... | collective-permute-start | bytes 1544 | tf_op jit(solution)/shard_map/ppermute | solution.py:276
  27.7 47.4 %collective-permute-start.4 = (f32[1,128]{1,0:T(1,128)S(1)}, f32[1,128]{1,0:T(1,128)S(1)}, u32[]{:S(2)}, u32[]{:S(2)}) collective-permute-start(f32[1,128]{1,0:T(1,128)S(1)} %get-tuple-element.32), channel_id=1, source_target_pairs={{31,0},{28,1},{29,2},{30,3},{3,4},{0,5},{1,6},{2,7},{7,8},{4,9},{5... | collective-permute-start | bytes 1544 | tf_op jit(solution)/shard_map/ppermute | solution.py:276
  28.3 46.8 %collective-permute-start.2 = (f32[120,256]{1,0:T(8,128)S(1)}, f32[120,256]{1,0:T(8,128)S(1)}, u32[]{:S(2)}, u32[]{:S(2)}) collective-permute-start(f32[120,256]{1,0:T(8,128)S(1)} %get-tuple-element.27), channel_id=1, source_target_pairs={{3,0},{0,1},{1,2},{2,3},{7,4},{4,5},{5,6},{6,7},{11,8},{8,9},{9,10... | collective-permute-start | bytes 368648 | tf_op jit(solution)/shard_map/ppermute | solution.py:272
  31.1 44.0 %collective-permute-start.3 = (f32[120,256]{1,0:T(8,128)S(1)}, f32[120,256]{1,0:T(8,128)S(1)}, u32[]{:S(2)}, u32[]{:S(2)}) collective-permute-start(f32[120,256]{1,0:T(8,128)S(1)} %get-tuple-element.28), channel_id=1, source_target_pairs={{1,0},{2,1},{3,2},{0,3},{5,4},{6,5},{7,6},{4,7},{9,8},{10,9},{11,1... | collective-permute-start | bytes 368648 | tf_op jit(solution)/shard_map/ppermute | solution.py:272

commit v2 on v1

--- a/solution.py
+++ b/solution.py
@@ -1,3 +1,5 @@
+import functools
+
 import jax
 import jax.numpy as jnp
 import numpy as np
@@ -49,6 +51,17 @@
     return high, low
 
 
+def repeat(count, width, work):
+    def several(k, _):
+        for u in range(width):
+            work(k * width + u)
+        return 0
+
+    lax.fori_loop(0, count // width, several, 0)
+    for i in range(count // width * width, count):
+        work(i)
+
+
 def sum_cols(g):
     n = g.shape[-1]
     col = lax.broadcasted_iota(jnp.int32, g.shape, 1)
@@ -107,7 +120,7 @@
         values = [stiff[k, k + d] if 0 <= k + d < 4 else 0.0 for k in range(4)]
         coefs.append((d, by_node(sub, values)))
 
-    def level(i, _):
+    def level(i):
         index = step * chunk + i
         f = air[i].reshape(rows // TILE, TILE, cols)
         across = jnp.zeros_like(f)
@@ -124,13 +137,12 @@
         row_lo[pl.ds(index, 1), :] = local[0:1, :]
         row_hi[pl.ds(index, 1), :] = local[rows - 1 :, :]
         summed[i] = sum_rows(sum_cols(local))
-        return 0
-
-    lax.fori_loop(0, chunk, level, 0, unroll=2 if chunk % 2 == 0 else 1)
+
+    repeat(chunk, 4, level)
 
 
 def softplus2(y):
-    return jnp.maximum(y, 0.0) + jnp.log2(1.0 + jnp.exp2(-jnp.abs(y)))
+    return jnp.maximum(y, jnp.log2(1.0 + jnp.exp2(jnp.minimum(y, 100.0))))
 
 
 def physics_kernel(flag, mixing, air, out, y, csum):
@@ -163,7 +175,7 @@
                 y[r] = value - jnp.dot(acat, stack, preferred_element_type=F32)
             return carry
 
-        lax.fori_loop(0, SUBSTEPS, substep, 0)
+        lax.fori_loop(0, SUBSTEPS, substep, 0, unroll=4)
         mhigh, mlow = split(0.25 * mix)
         mcat = jnp.concatenate([mhigh, mhigh, mlow], axis=1)
         for r in range(rows):
@@ -175,9 +187,53 @@
             out[1, :, r, :] = -0.25 * total[:levels]
 
 
+def edge_kernel(
+    nx, ny, col_lo, col_hi, row_lo, row_hi, edge_l, edge_r, edge_b, edge_a,
+    cols_in, rows_in, corners_in, send, recv,
+):
+    rows = col_lo.shape[0]
+    x, y = lax.axis_index("fx"), lax.axis_index("fy")
+    west, east = lax.rem(x + nx - 1, nx), lax.rem(x + 1, nx)
+    south, north = lax.rem(y + ny - 1, ny), lax.rem(y + 1, ny)
+    around = [
+        (west, y), (east, y), (x, south), (x, north),
+        (west, south), (west, north), (east, south), (east, north),
+    ]
+    barrier = pltpu.get_barrier_semaphore()
+    for device in around:
+        pl.semaphore_signal(
+            barrier, inc=1, device_id=device, device_id_type=pl.DeviceIdType.MESH
+        )
+    pl.semaphore_wait(barrier, len(around))
+    first, last = pl.ds(0, TILE), pl.ds(rows - TILE, TILE)
+    moves = [
+        (row_hi, rows_in.at[0], around[3]),
+        (row_lo, rows_in.at[1], around[2]),
+        (col_hi, cols_in.at[0], around[1]),
+        (col_lo, cols_in.at[1], around[0]),
+        (col_hi.at[last], corners_in.at[0], around[7]),
+        (col_hi.at[first], corners_in.at[1], around[6]),
+        (col_lo.at[last], corners_in.at[2], around[5]),
+        (col_lo.at[first], corners_in.at[3], around[4]),
+    ]
+    copies = []
+    for k, (source, target, device) in enumerate(moves):
+        copy = pltpu.make_async_remote_copy(
+            src_ref=source, dst_ref=target, send_sem=send.at[k], recv_sem=recv.at[k],
+            device_id=device, device_id_type=pl.DeviceIdType.MESH,
+        )
+        copy.start()
+        copies.append(copy)
+    for copy in copies:
+        copy.wait()
+    edge_l[...] = sum_rows(cols_in[0], corners_in[0, TILE - 1 :, :], corners_in[1, :1, :])
+    edge_r[...] = sum_rows(cols_in[1], corners_in[2, TILE - 1 :, :], corners_in[3, :1, :])
+    edge_b[...] = sum_cols(rows_in[0])
+    edge_a[...] = sum_cols(rows_in[1])
+
+
 def final_kernel(
-    flag, air, summed, phys, msum, left, right, below, above, lb, la, rb, ra, out,
-    inv, edge_l, edge_r, edge_b, edge_a,
+    flag, air, summed, phys, msum, edge_l, edge_r, edge_b, edge_a, out, inv
 ):
     step = pl.program_id(0)
     chunk, rows, cols = air.shape
@@ -195,22 +251,17 @@
 
     @pl.when(step == 0)
     def _():
-        edge_l[...] = sum_rows(left[...], lb[...], la[...])
-        edge_r[...] = sum_rows(right[...], rb[...], ra[...])
-        edge_b[...] = sum_cols(below[...])
-        edge_a[...] = sum_cols(above[...])
         inv[...] = 0.05 / full(msum[...], pl.num_programs(0) * chunk)
 
     def levels_with(extra):
-        def level(i, _):
+        def level(i):
             total = full(summed[i], step * chunk + i)
             value = air[i] + inv[...] * total
             if extra:
                 value = value + phys[i]
             out[i] = value
-            return 0
-
-        lax.fori_loop(0, chunk, level, 0)
+
+        repeat(chunk, 4, level)
 
     @pl.when(flag[0] > 0)
     def _():
@@ -263,22 +314,22 @@
 
     nx, ny = lax.axis_size("fx"), lax.axis_size("fy")
 
-    def shifted(value, dx, dy):
-        if dy == 0:
-            pairs = [((i + dx) % nx, i) for i in range(nx)]
-            return lax.ppermute(value, "fx", pairs)
-        if dx == 0:
-            pairs = [((j + dy) % ny, j) for j in range(ny)]
-            return lax.ppermute(value, "fy", pairs)
-        pairs = [
-            (((i + dx) % nx) * ny + (j + dy) % ny, i * ny + j) for i in range(nx) for j in range(ny)
-        ]
-        return lax.ppermute(value, ("fx", "fy"), pairs)
-
-    left, right = shifted(col_hi, -1, 0), shifted(col_lo, 1, 0)
-    below, above = shifted(row_hi, 0, -1), shifted(row_lo, 0, 1)
-    lb, la = shifted(col_hi[rows - 1 :], -1, -1), shifted(col_hi[:1], -1, 1)
-    rb, ra = shifted(col_lo[rows - 1 :], 1, -1), shifted(col_lo[:1], 1, 1)
+    vmem = pl.BlockSpec(memory_space=pltpu.VMEM)
+    edges = pl.pallas_call(
+        functools.partial(edge_kernel, nx, ny),
+        out_shape=[edge_col, edge_col, edge_row, edge_row],
+        in_specs=[vmem] * 4,
+        out_specs=[vmem] * 4,
+        scratch_shapes=[
+            pltpu.VMEM((2, rows, LANES), F32),
+            pltpu.VMEM((2, row_slots, cols), F32),
+            pltpu.VMEM((4, TILE, LANES), F32),
+            pltpu.SemaphoreType.DMA((8,)),
+            pltpu.SemaphoreType.DMA((8,)),
+        ],
+        compiler_params=pltpu.CompilerParams(collective_id=0, has_side_effects=True),
+        name="edge_exchange",
+    )(col_lo, col_hi, row_lo, row_hi)
 
     depth = -(-levels // 16) * 16
     mix = jnp.zeros((depth, depth), F32).at[:levels, :levels].set(mixing)
@@ -315,21 +366,16 @@
                 plane_spec, plane_spec, phys_spec, whole((rows, cols)),
                 whole((rows, LANES)), whole((rows, LANES)),
                 whole((row_slots, cols)), whole((row_slots, cols)),
-            ] + [whole((1, LANES))] * 4,
+            ],
             out_specs=plane_spec,
             scratch_shapes=[
                 pltpu.VMEM((rows, cols), F32),
-                pltpu.VMEM((rows, LANES), F32),
-                pltpu.VMEM((rows, LANES), F32),
-                pltpu.VMEM((row_slots, cols), F32),
-                pltpu.VMEM((row_slots, cols), F32),
             ],
         ),
         out_shape=plane,
         compiler_params=pltpu.CompilerParams(vmem_limit_bytes=32 * 2**20),
         name="step_sum",
-    )(flag, flat, summed, phys.reshape(planes, rows, cols), msum, left, right, below, above,
-      lb, la, rb, ra)
+    )(flag, flat, summed, phys.reshape(planes, rows, cols), msum, *edges)
     return result.reshape(air_state.shape)
 
 

time: 87.4 us -> 75.6 us (0.86)
  the two profiles are of different devices: /device:TPU:8 before, /device:TPU:0 now
where the time goes in v2:
time: 75.6 us; the launch traced here: 74.4 us
  Pallas kernels  55.2 us (73%)
  local copies, waits for them, and re-layouts  18.5 us (24%)
    pallas_call x1, Pallas kernels, body(): pl.pallas_call(functools.partial(edge_kernel, nx, ny), out_shape=[edge_co...  41.7 us
    unnamed x36, local copies, waits for them, and re-layouts  17.7 us
    pallas_call x1, Pallas kernels, body(): pl.pallas_call(local_kernel, grid=(steps,), out_shape=[plane, jax.ShapeDt...  8.48 us
    pallas_call x1, Pallas kernels, body(): pl.pallas_call(final_kernel, grid_spec=pltpu.PrefetchScalarGridSpec(num_s...  4.7 us

profile of v2, /device:TPU:0, one launch (start us, length us, event | category | flops | bytes accessed | tf_op | source)
XLA Modules:
  0.0 74.4 jit_solution(15782912720702094214)
XLA Ops:
  0.7 0.8 %scatter.4.mixing = f32[64,64]{1,0:T(8,128)S(1)} pad(f32[58,58]{1,0:T(8,128)} %param.12, f32[]{:T(128)} %constant.34.clone.1), padding=0_6x0_6 | pad | bytes 29844 | tf_op jit(solution)/shard_map/scatter | solution.py:335
  1.4 2.1 %copy-done = f32[2,58,32,256]{3,2,1,0:T(8,128)S(1)} copy-done((f32[2,58,32,256]{3,2,1,0:T(8,128)S(1)}, f32[2,58,32,256]{3,2,1,0:T(8,128)}, u32[]{:S(2)}) %copy-start) | copy-done | bytes 3801112
  3.5 0.3 column_physics.1
  3.8 0.0 copy-start.2
  3.8 1.8 %copy-done.2 = f32[2,58,32,256]{3,2,1,0:T(8,128)} copy-done((f32[2,58,32,256]{3,2,1,0:T(8,128)}, f32[2,58,32,256]{3,2,1,0:T(8,128)S(1)}, u32[]{:S(2)}) %copy-start.2) | copy-done | bytes 3801112
  5.6 0.0 copy-done.6
  5.7 0.0 copy-done.12
  5.7 8.5 %local_terms.1 = (f32[116,32,256]{2,1,0:T(8,128)S(1)}, f32[32,256]{1,0:T(8,128)S(1)}, f32[32,128]{1,0:T(8,128)S(1)}, f32[32,128]{1,0:T(8,128)S(1)}, f32[120,256]{1,0:T(8,128)S(1)}, /*index=5*/f32[120,256]{1,0:T(8,128)S(1)}) custom-call(f32[116,32,256]{2,1,0:T(8,128)S(1)} %bitcast.5, f32[32,256]{1,0:T(8,128)S(1)} %copy-done.12, f32[32,256]{1,0:T(8,128)S(1)} %copy-done.13, ...), custom_call_target="tpu_custom_call" | custom-call | tf_op jit(solution)/shard_map/local_terms/pallas_call | solution.py:295
  14.2 0.0 copy-start.4
  14.2 1.9 %copy-done.4 = f32[116,32,256]{2,1,0:T(8,128)} copy-done((f32[116,32,256]{2,1,0:T(8,128)}, f32[116,32,256]{2,1,0:T(8,128)S(1)}, u32[]{:S(2)}) %copy-start.4) | copy-done | bytes 3801112
  16.0 0.6 copy-done.8
  16.7 0.7 copy-done.9
  17.3 0.6 copy-done.14
  17.9 0.6 copy-done.15
  18.5 41.7 %edge_exchange.1 = (f32[32,128]{1,0:T(8,128)}, f32[32,128]{1,0:T(8,128)}, f32[120,256]{1,0:T(8,128)}, f32[120,256]{1,0:T(8,128)}) custom-call(f32[32,128]{1,0:T(8,128)} %copy-done.14, f32[32,128]{1,0:T(8,128)} %copy-done.15, f32[120,256]{1,0:T(8,128)} %copy-done.8, f32[120,256]{1,0:T(8,128)} %copy-done.9), custom_call_target="tpu_custom_call" | custom-call | tf_op jit(solution)/shard_map/edge_exchange/pallas_call | solution.py:318
  60.2 0.0 copy-start.1
  60.2 2.1 %copy-done.1 = f32[2,58,32,256]{3,2,1,0:T(8,128)S(1)} copy-done((f32[2,58,32,256]{3,2,1,0:T(8,128)S(1)}, f32[2,58,32,256]{3,2,1,0:T(8,128)}, u32[]{:S(2)}) %copy-start.1) | copy-done | bytes 3801112
  62.3 2.1 %copy-done.3 = f32[2,58,32,256]{3,2,1,0:T(8,128)S(1)} copy-done((f32[2,58,32,256]{3,2,1,0:T(8,128)S(1)}, f32[2,58,32,256]{3,2,1,0:T(8,128)}, u32[]{:S(2)}) %copy-start.3) | copy-done | bytes 3801112
  64.4 2.1 %copy-done.5 = f32[116,32,256]{2,1,0:T(8,128)S(1)} copy-done((f32[116,32,256]{2,1,0:T(8,128)S(1)}, f32[116,32,256]{2,1,0:T(8,128)}, u32[]{:S(2)}) %copy-start.5) | copy-done | bytes 3801112
  66.5 0.9 %copy-done.10 = f32[120,256]{1,0:T(8,128)S(1)} copy-done((f32[120,256]{1,0:T(8,128)S(1)}, f32[120,256]{1,0:T(8,128)}, u32[]{:S(2)}) %copy-start.10) | copy-done | bytes 122904
  67.4 0.9 %copy-done.11 = f32[120,256]{1,0:T(8,128)S(1)} copy-done((f32[120,256]{1,0:T(8,128)S(1)}, f32[120,256]{1,0:T(8,128)}, u32[]{:S(2)}) %copy-start.11) | copy-done | bytes 122904
  68.3 0.7 copy-done.16
  69.0 0.7 copy-done.17
  69.7 4.7 %step_sum.1 = f32[116,32,256]{2,1,0:T(8,128)} custom-call(s32[1]{0:T(128)} %bitcast.flag, f32[116,32,256]{2,1,0:T(8,128)S(1)} %bitcast.6, f32[116,32,256]{2,1,0:T(8,128)S(1)} %copy-done.5, f32[116,32,256]{2,1,0:T(8,128)S(1)} %bitcast.7, f32[32,256]{1,0:T(8,128)S(1)} %get-tuple-element.28.msum, f32[32,128]{1,0:T(8,128)S(1)} %copy-done.16, ...), custom_call_target="tpu_custom_call" | custom-call | tf_op jit(solution)/shard_map/step_sum/pallas_call | solution.py:360
  (17 shorter events, 0.0 us)
Async XLA Ops:
  1.4 2.1 %copy-start = (f32[2,58,32,256]{3,2,1,0:T(8,128)S(1)}, f32[2,58,32,256]{3,2,1,0:T(8,128)}, u32[]{:S(2)}) copy-start(f32[2,58,32,256]{3,2,1,0:T(8,128)} %air.1) | copy-start | bytes 11403268
  3.5 2.2 %copy-start.6 = (bf16[256,256]{1,0:T(8,128)(2,1)S(1)}, bf16[256,256]{1,0:T(8,128)(2,1)}, u32[]{:S(2)}) copy-start(bf16[256,256]{1,0:T(8,128)(2,1)} %constant.36.clone.klo) | copy-start | bytes 393220
  3.5 2.2 %copy-start.7 = (bf16[256,256]{1,0:T(8,128)(2,1)S(1)}, bf16[256,256]{1,0:T(8,128)(2,1)}, u32[]{:S(2)}) copy-start(bf16[256,256]{1,0:T(8,128)(2,1)} %constant.35.clone.khi) | copy-start | bytes 393220
  3.5 2.2 %copy-start.12 = (f32[32,256]{1,0:T(8,128)S(1)}, f32[32,256]{1,0:T(8,128)}, u32[]{:S(2)}) copy-start(f32[32,256]{1,0:T(8,128)} %jac.1) | copy-start | bytes 98308
  3.5 2.2 %copy-start.13 = (f32[32,256]{1,0:T(8,128)S(1)}, f32[32,256]{1,0:T(8,128)}, u32[]{:S(2)}) copy-start(f32[32,256]{1,0:T(8,128)} %visc.1) | copy-start | bytes 98308
  3.8 1.8 %copy-start.2 = (f32[2,58,32,256]{3,2,1,0:T(8,128)}, f32[2,58,32,256]{3,2,1,0:T(8,128)S(1)}, u32[]{:S(2)}) copy-start(f32[2,58,32,256]{3,2,1,0:T(8,128)S(1)} %column_physics.1) | copy-start | bytes 11403268
  14.2 1.9 %copy-start.4 = (f32[116,32,256]{2,1,0:T(8,128)}, f32[116,32,256]{2,1,0:T(8,128)S(1)}, u32[]{:S(2)}) copy-start(f32[116,32,256]{2,1,0:T(8,128)S(1)} %get-tuple-element.27.summed) | copy-start | bytes 11403268
  16.0 0.7 copy-start.8
  16.7 0.7 copy-start.9
  17.3 0.6 copy-start.14
  17.9 0.6 copy-start.15
  60.2 2.1 %copy-start.1 = (f32[2,58,32,256]{3,2,1,0:T(8,128)S(1)}, f32[2,58,32,256]{3,2,1,0:T(8,128)}, u32[]{:S(2)}) copy-start(f32[2,58,32,256]{3,2,1,0:T(8,128)} %air.1) | copy-start | bytes 11403268
  62.3 2.1 %copy-start.3 = (f32[2,58,32,256]{3,2,1,0:T(8,128)S(1)}, f32[2,58,32,256]{3,2,1,0:T(8,128)}, u32[]{:S(2)}) copy-start(f32[2,58,32,256]{3,2,1,0:T(8,128)} %copy-done.2) | copy-start | bytes 11403268
  64.4 2.1 %copy-start.5 = (f32[116,32,256]{2,1,0:T(8,128)S(1)}, f32[116,32,256]{2,1,0:T(8,128)}, u32[]{:S(2)}) copy-start(f32[116,32,256]{2,1,0:T(8,128)} %copy-done.4) | copy-start | bytes 11403268
  66.5 0.9 %copy-start.10 = (f32[120,256]{1,0:T(8,128)S(1)}, f32[120,256]{1,0:T(8,128)}, u32[]{:S(2)}) copy-start(f32[120,256]{1,0:T(8,128)} %get-tuple-element.35.edge_b) | copy-start | bytes 368644
  67.4 0.9 %copy-start.11 = (f32[120,256]{1,0:T(8,128)S(1)}, f32[120,256]{1,0:T(8,128)}, u32[]{:S(2)}) copy-start(f32[120,256]{1,0:T(8,128)} %get-tuple-element.36.edge_a) | copy-start | bytes 368644
  68.3 0.7 copy-start.16
  69.0 0.7 copy-start.17
